TPU v7x, 128 devices: a whole 4x4x4 slice. The times are simulated.
128 devices in a mesh: gx: 32 (over z, y_lo, x), gy: 4 (over y_hi, core).
Axes of the slice: x: 4, y: 4 (y_hi: 2, y_lo: 2; y = y_hi * 2 + y_lo), z: 4, core: 2. Of those that a mesh axis runs over, the one named last changes fastest.
Arguments:
- fluid_source: float32 [256, 128, 512], P('gx', 'gy'), may hold values from -6 to 6
- fluid_diag: float32 [256, 128, 512], P('gx', 'gy'), may hold values from 0.05 to 2
- stiff_ref: float32 [81, 81], replicated
- elem_coef: float32 [49152], P(('gx', 'gy')), may hold values from 0.3 to 3
- connect: int32 [27, 49152], P(None, ('gx', 'gy')), may hold values from 0 to 12543
- live_count: int32 [128], P(('gx', 'gy')), may hold values from 48 to 384, as said below
- node_mass: float32 [393216], P(('gx', 'gy')), may hold values from 0.5 to 2
- solid_load: float32 [3, 393216], P(None, ('gx', 'gy')), may hold values from -24 to 24
- wet_normal: float32 [3, 32768], P(None, ('gx', 'gy')), may hold values from -6 to 6
- trac_face: int32 [4, 32768], P(None, ('gx', 'gy')), may hold values from 0 to 1023
- trac_weight: float32 [4, 32768], P(None, ('gx', 'gy')), may hold values from 0 to 0.5
- wall_node: int32 [4, 256, 128], P(None, 'gx', 'gy'), may hold values from 0 to 1023
- wall_weight: float32 [4, 256, 128], P(None, 'gx', 'gy'), may hold values from 0 to 0.5
Outputs:
- pressure: float32 [256, 128, 512], P('gx', 'gy')
- displacement: float32 [3, 393216], P(None, ('gx', 'gy'))
Inputs may be any that keep to these rules, and one draw needn't show every extreme that they name: `connect`: entries number columns of the extended node list of the element's segment: its 12288 own nodes, then the first 256 nodes of the next segment. `live_count`: live slots of each device come first in its 384 slots; some device is full. `trac_face`: indices into the wall faces of the node's span slab, in the order of wall_seg. `wall_node`: indices into the face's segment's list of 1024 wetted nodes.
All inputs are finite; a program needn't handle non-finite values.
Results may differ from a plain program's by a relative error of at most 0.00014.
Values sent between devices are 32-bit elements; how exact they have to be, the bound alone decides.
No kernel may reach another device: no remote copies, remote signals or barrier semaphores. Data moves between devices by JAX's collectives and lax.ppermute only.
A program may use at most 64 MiB of HBM per device.

v0:
```python
import jax
import jax.numpy as jnp
from jax import lax
from jax.sharding import PartitionSpec as P

PLANE = 256
BLK = 384
ITERS = 2
PSEUDO = 2
COUPLE = 2
pseudo_weight = 0.8
traction_scale = 30.0
motion_scale = 2.0
relax_weight = 0.5


def padded_2(block, sides, width):
    for axis, dim in sides:
        count = lax.axis_size(axis)
        forward = [(i, i + 1) for i in range(count - 1)]
        backward = [(target, source) for source, target in forward]
        low = lax.ppermute(
            lax.slice_in_dim(block, block.shape[dim] - width, None, axis=dim), axis, forward
        )
        high = lax.ppermute(lax.slice_in_dim(block, 0, width, axis=dim), axis, backward)
        block = jnp.concatenate([low, block, high], axis=dim)
    return block


def from_behind(value, axis, by):
    length = lax.axis_size(axis)
    pairs = [(i, i + by) for i in range(length) if 0 <= i + by < length]
    return lax.ppermute(value, axis, pairs)


def fluid_step(pressure, fluid_diag, forcing):
    framed = padded_2(pressure, (("gx", 0), ("gy", 1)), 1)
    padded = jnp.pad(framed, ((0, 0), (0, 0), (1, 1)))
    beside = padded[2:, 1:-1, 1:-1] + padded[:-2, 1:-1, 1:-1]
    beside = beside + padded[1:-1, 2:, 1:-1] + padded[1:-1, :-2, 1:-1]
    beside = beside + padded[1:-1, 1:-1, 2:] + padded[1:-1, 1:-1, :-2]
    center = 6.0 + fluid_diag
    applied = center * pressure - beside
    return pressure + pseudo_weight * (forcing - applied) / center


def global_sums(values):
    totals = lax.psum((values[0],), ("gx", "gy"))
    return totals


def conjugate(apply_fn, solid_force):
    solution = jnp.zeros_like(solid_force)
    residual = solid_force
    direction = residual
    norm_now = global_sums((jnp.sum(residual * residual),))[0]
    for iteration in range(ITERS):
        applied = apply_fn(direction)
        curvature = global_sums((jnp.sum(direction * applied),))[0]
        step_size = norm_now / curvature
        solution = solution + step_size * direction
        residual = residual - step_size * applied
        norm_next = global_sums((jnp.sum(residual * residual),))[0]
        direction = residual + norm_next / norm_now * direction
        norm_now = norm_next
    return solution


def local(
    fluid_source,
    fluid_diag,
    stiff_ref,
    elem_coef,
    connect,
    live_count,
    node_mass,
    solid_load,
    wet_normal,
    trac_face,
    trac_weight,
    wall_node,
    wall_weight,
):
    owned_nodes = node_mass.shape[0]
    wet_count = wet_normal.shape[1]
    elem_count = connect.shape[1]
    node_order = connect.shape[0]
    chord_parts = lax.axis_size("gy")
    seg_nodes = owned_nodes * chord_parts
    turn_width = BLK
    live_here = live_count[0]
    position = jnp.arange(elem_count, dtype=jnp.int32)
    elem_weight = elem_coef * (position < live_here).astype(jnp.float32)
    turn_count = elem_count // turn_width

    def element_terms(extended):

        def one_turn(turn_index, summed):
            gathered = extended[:, connect].reshape(3 * node_order, turn_width)
            product = jnp.dot(
                stiff_ref,
                gathered,
                precision=lax.Precision.HIGHEST,
                preferred_element_type=jnp.float32,
            )
            product = product * elem_weight[None, :]
            return summed.at[:, connect].add(product.reshape(3, node_order, turn_width))

        return lax.fori_loop(0, turn_count, one_turn, jnp.zeros(extended.shape, jnp.float32))

    def plane_terms(segment_vec):
        following = from_behind(segment_vec[:, :PLANE], "gx", -1)
        summed = element_terms(jnp.concatenate([segment_vec, following], axis=1))
        tail_part = from_behind(summed[:, seg_nodes:], "gx", 1)
        return summed[:, :seg_nodes].at[:, :PLANE].add(tail_part)

    def apply_fn(vector_in):
        segment_vec = lax.all_gather(vector_in, "gy", axis=1, tiled=True)
        return (
            lax.psum_scatter(plane_terms(segment_vec), "gy", scatter_dimension=1, tiled=True)
            + node_mass[None, :] * vector_in
        )

    displacement = jnp.zeros(solid_load.shape, jnp.float32)
    pressure = jnp.zeros(fluid_source.shape, jnp.float32)
    for coupling in range(COUPLE):
        motion = jnp.sum(wet_normal * displacement[:, :wet_count], axis=0)
        motion_all = lax.all_gather(motion, "gy", axis=0, tiled=True)
        wall_source = motion_scale * jnp.sum(wall_weight * motion_all[wall_node], axis=0)
        forcing = fluid_source.at[:, :, 0].add(wall_source)
        for pseudo_step in range(PSEUDO):
            pressure = fluid_step(pressure, fluid_diag, forcing)
        wall_all = lax.all_gather(pressure[:, :, 0].reshape(-1), "gy", axis=0, tiled=True)
        traction = jnp.sum(trac_weight * wall_all[trac_face], axis=0)
        solid_force = solid_load.at[:, :wet_count].add(
            traction_scale * traction[None, :] * wet_normal
        )
        solution = conjugate(apply_fn, solid_force)
        displacement = displacement + relax_weight * (solution - displacement)
    return (pressure, displacement)


def solution(mesh):
    in_specs = (
        P("gx", "gy", None),
        P("gx", "gy", None),
        P(),
        P(("gx", "gy")),
        P(None, ("gx", "gy")),
        P(("gx", "gy")),
        P(("gx", "gy")),
        P(None, ("gx", "gy")),
        P(None, ("gx", "gy")),
        P(None, ("gx", "gy")),
        P(None, ("gx", "gy")),
        P(None, "gx", "gy"),
        P(None, "gx", "gy"),
    )
    out_specs = (P("gx", "gy", None), P(None, ("gx", "gy")))
    return jax.shard_map(local, mesh=mesh, in_specs=in_specs, out_specs=out_specs, check_vma=False)
```

profile of v0, /device:TPU:1, one launch (start us, length us, event | category | flops | bytes accessed | tf_op | source)
XLA Modules:
  0.0 1283.9 jit_solution(11407972666191639603)
XLA Ops:
  16.6 7.8 all-gather
  31.3 5.0 collective-permute-start.3
  46.7 6.8 collective-permute-start.7
  56.0 6.6 all-gather.1
  67.9 7.5 all_gather.26
  84.6 22.8 %gather_fusion.2 = f32[10368,3]{1,0:T(8,128)} fusion(f32[3,12544]{0,1:T(8,128)} %copy.164, s32[11264]{0:T(1024)S(1)} %pad_clamp_fusion), kind=kCustom, calls=%fused_computation.2 | custom fusion | bytes 290304 | tf_op jit(solution)/shard_map/while/body/eval_jaxpr/gather | solution.py:99
  115.6 61.1 %scatter_custom_fusion = f32[3,12544]{0,1:T(8,128)} fusion(s32[10368]{0:T(1024)S(1)} %reshape.330, f32[10368,3]{1,0:T(8,128)} %bitcast.64, f32[]{:T(128)} %constant.216.clone.1), kind=kCustom, calls=%fused_computation.18 | custom fusion | flops 31104 | bytes 151040 | tf_op jit(solution)/shard_map/while/body/eval_jaxpr/scatter-add | solution.py:107
  181.9 4.7 slice.442
  188.9 77.8 %reduce-scatter.13.cloned.1.call-done = f32[3072,3]{1,0:T(8,128)} async-done(((f32[12288,3]{1,0:T(8,128)}), f32[3072,3]{1,0:T(8,128)}) %reduce-scatter.13.cloned.1.call-update) | async-done | bytes 36880
  269.4 65.1 %all-reduce.7 = (f32[]{:T(128)}, f32[]{:T(128)}) all-reduce(f32[]{:T(128)} %get-tuple-element.181, f32[]{:T(128)} %get-tuple-element.180), channel_id=1, replica_groups=mesh['gx'=32,'gy'=4] {'gx','gy'}, use_global_device_ids=true, to_apply=%region_5.6 | all-reduce | flops 2 | bytes 16 | tf_op jit(solution)/shard_map/psum | solution.py:48
  336.3 64.3 %psum.58 = f32[]{:T(128)} all-reduce(f32[]{:T(128)} %multiply_reduce_fusion.5), channel_id=1, replica_groups=mesh['gx'=32,'gy'=4] {'gx','gy'}, use_global_device_ids=true, to_apply=%region_12.13 | all-reduce | flops 1 | bytes 8 | tf_op jit(solution)/shard_map/psum | solution.py:48
  401.9 7.9 all_gather.27
  418.4 22.8 %gather_fusion.3 = f32[10368,3]{1,0:T(8,128)} fusion(f32[3,12544]{0,1:T(8,128)} %copy.168, s32[11264]{0:T(1024)S(1)} %pad_clamp_fusion), kind=kCustom, calls=%fused_computation.3 | custom fusion | bytes 290304 | tf_op jit(solution)/shard_map/while/body/eval_jaxpr/gather | solution.py:99
  449.4 61.1 %scatter_custom_fusion.1 = f32[3,12544]{0,1:T(8,128)} fusion(s32[10368]{0:T(1024)S(1)} %reshape.330, f32[10368,3]{1,0:T(8,128)} %bitcast.65, f32[]{:T(128)} %constant.216.clone.1), kind=kCustom, calls=%fused_computation.16 | custom fusion | flops 31104 | bytes 151040 | tf_op jit(solution)/shard_map/while/body/eval_jaxpr/scatter-add | solution.py:107
  513.1 4.7 slice.446
  534.3 52.5 %reduce-scatter.15.cloned.1.call-done = f32[3072,3]{1,0:T(8,128)} async-done(((f32[12288,3]{1,0:T(8,128)}), f32[3072,3]{1,0:T(8,128)}) %reduce-scatter.15.cloned.1.call-update) | async-done | bytes 36880
  589.9 65.1 %psum.59 = f32[]{:T(128)} all-reduce(f32[]{:T(128)} %multiply_reduce_fusion.4), channel_id=1, replica_groups=mesh['gx'=32,'gy'=4] {'gx','gy'}, use_global_device_ids=true, to_apply=%region_16.17 | all-reduce | flops 1 | bytes 8 | tf_op jit(solution)/shard_map/psum | solution.py:48
  656.4 7.0 all-gather.2
  684.5 7.0 all-gather.3
  696.8 7.6 all_gather.30
  713.4 22.8 %gather_fusion.6 = f32[10368,3]{1,0:T(8,128)} fusion(f32[3,12544]{0,1:T(8,128)} %copy.173, s32[11264]{0:T(1024)S(1)} %pad_clamp_fusion), kind=kCustom, calls=%fused_computation.6 | custom fusion | bytes 290304 | tf_op jit(solution)/shard_map/while/body/eval_jaxpr/gather | solution.py:99
  744.4 61.1 %scatter_custom_fusion.2 = f32[3,12544]{0,1:T(8,128)} fusion(s32[10368]{0:T(1024)S(1)} %reshape.330, f32[10368,3]{1,0:T(8,128)} %bitcast.66, f32[]{:T(128)} %constant.216.clone.1), kind=kCustom, calls=%fused_computation.14 | custom fusion | flops 31104 | bytes 151040 | tf_op jit(solution)/shard_map/while/body/eval_jaxpr/scatter-add | solution.py:107
  809.8 4.7 slice.460
  816.8 71.2 %reduce-scatter.17.cloned.1.call-done = f32[3072,3]{1,0:T(8,128)} async-done(((f32[12288,3]{1,0:T(8,128)}), f32[3072,3]{1,0:T(8,128)}) %reduce-scatter.17.cloned.1.call-update) | async-done | bytes 36880
  890.6 65.1 %all-reduce.6 = (f32[]{:T(128)}, f32[]{:T(128)}) all-reduce(f32[]{:T(128)} %get-tuple-element.179, f32[]{:T(128)} %get-tuple-element.178), channel_id=1, replica_groups=mesh['gx'=32,'gy'=4] {'gx','gy'}, use_global_device_ids=true, to_apply=%region_21.22 | all-reduce | flops 2 | bytes 16 | tf_op jit(solution)/shard_map/psum | solution.py:48
  957.5 63.8 %psum.62 = f32[]{:T(128)} all-reduce(f32[]{:T(128)} %multiply_reduce_fusion.1), channel_id=1, replica_groups=mesh['gx'=32,'gy'=4] {'gx','gy'}, use_global_device_ids=true, to_apply=%region_27.28 | all-reduce | flops 1 | bytes 8 | tf_op jit(solution)/shard_map/psum | solution.py:48
  1022.6 7.9 all_gather.31
  1039.1 22.8 %gather_fusion.7 = f32[10368,3]{1,0:T(8,128)} fusion(f32[3,12544]{0,1:T(8,128)} %copy.177, s32[11264]{0:T(1024)S(1)} %pad_clamp_fusion), kind=kCustom, calls=%fused_computation.7 | custom fusion | bytes 290304 | tf_op jit(solution)/shard_map/while/body/eval_jaxpr/gather | solution.py:99
  1070.1 61.1 %scatter_custom_fusion.3 = f32[3,12544]{0,1:T(8,128)} fusion(s32[10368]{0:T(1024)S(1)} %reshape.330, f32[10368,3]{1,0:T(8,128)} %bitcast.63, f32[]{:T(128)} %constant.216.clone.1), kind=kCustom, calls=%fused_computation.12 | custom fusion | flops 31104 | bytes 151040 | tf_op jit(solution)/shard_map/while/body/eval_jaxpr/scatter-add | solution.py:107
  1133.8 4.7 slice.464
  1140.8 66.8 %reduce-scatter.19.cloned.1.call-done = f32[3072,3]{1,0:T(8,128)} async-done(((f32[12288,3]{1,0:T(8,128)}), f32[3072,3]{1,0:T(8,128)}) %reduce-scatter.19.cloned.1.call-update) | async-done | bytes 36880
  1210.1 65.0 %psum.63 = f32[]{:T(128)} all-reduce(f32[]{:T(128)} %multiply_reduce_fusion), channel_id=1, replica_groups=mesh['gx'=32,'gy'=4] {'gx','gy'}, use_global_device_ids=true, to_apply=%region_31.0 | all-reduce | flops 1 | bytes 8 | tf_op jit(solution)/shard_map/psum | solution.py:48
  (191 shorter events, 178.7 us)
Async XLA Ops:
  7.2 104.4 %copy-start = (f32[81,81]{1,0:T(8,128)S(1)}, f32[81,81]{1,0:T(8,128)}, u32[]{:S(2)}) copy-start(f32[81,81]{1,0:T(8,128)} %param.31) | copy-start | bytes 78736
  7.2 259.6 %reduce-scatter.13.cloned.1.call-start = ((), (), s32[]{:S(2)}) async-start(), calls=%async_computation.4 | async-start | bytes 7864320
  9.1 20.0 %collective-permute-start = (f32[1,32,512]{2,1,0:T(8,128)S(1)}, f32[1,32,512]{2,1,0:T(8,128)S(1)}, u32[]{:S(2)}, u32[]{:S(2)}) collective-permute-start(f32[1,32,512]{2,1,0:T(8,128)S(1)} %broadcast.217), channel_id=1, source_target_pairs={{4,0},{8,4},{12,8},{16,12},{20,16},{24,20},{28,24},{32,28},{36,32}... | collective-permute-start | bytes 196616 | tf_op jit(solution)/shard_map/ppermute | solution.py:25
  10.4 18.7 %collective-permute-start.1 = (f32[1,32,512]{2,1,0:T(8,128)S(1)}, f32[1,32,512]{2,1,0:T(8,128)S(1)}, u32[]{:S(2)}, u32[]{:S(2)}) collective-permute-start(f32[1,32,512]{2,1,0:T(8,128)S(1)} %broadcast.217), channel_id=1, source_target_pairs={{0,4},{4,8},{8,12},{12,16},{16,20},{20,24},{24,28},{28,32},{32,36}... | collective-permute-start | bytes 196616 | tf_op jit(solution)/shard_map/ppermute | solution.py:22
  29.2 7.4 collective-permute-start.2
  31.3 5.9 collective-permute-start.3
  37.6 39.0 %copy-start.9 = (f32[384]{0:T(512)S(1)}, f32[384]{0:T(512)}, u32[]{:S(2)}) copy-start(f32[384]{0:T(512)} %param.32) | copy-start | bytes 4612
  38.1 5.3 collective-permute-start.4
  39.4 5.3 collective-permute-start.5
  44.8 10.1 collective-permute-start.6
  46.7 8.2 collective-permute-start.7
  75.3 5.0 collective-permute-start.8
  177.6 9.0 collective-permute-start.9
  186.7 82.0 %copy-start.3 = (f32[3072]{0:T(1024)S(1)}, f32[3072]{0:T(1024)}, u32[]{:S(2)}) copy-start(f32[3072]{0:T(1024)} %param.35) | copy-start | bytes 36868
  188.9 397.9 %reduce-scatter.15.cloned.1.call-start = ((), (), s32[]{:S(2)}) async-start(), calls=%async_computation.5 | async-start | bytes 7864320
  409.7 4.3 collective-permute-start.10
  511.4 6.4 collective-permute-start.11
  520.1 367.9 %reduce-scatter.17.cloned.1.call-start = ((), (), s32[]{:S(2)}) async-start(), calls=%async_computation.6 | async-start | bytes 7864320
  520.1 5.3 collective-permute-start.12
  521.4 5.3 collective-permute-start.13
  526.8 62.6 %collective-permute-start.14 = (f32[10,1,512]{2,1,0:T(1,128)S(1)}, f32[10,1,512]{2,1,0:T(1,128)S(1)}, u32[]{:S(2)}, u32[]{:S(2)}) collective-permute-start(f32[10,1,512]{2,1,0:T(1,128)S(1)} %get-tuple-element.189), channel_id=1, source_target_pairs={{1,0},{2,1},{3,2},{5,4},{6,5},{7,6},{9,8},{10,9},{11,10},{13,12},{... | collective-permute-start | bytes 61448 | tf_op jit(solution)/shard_map/ppermute | solution.py:25
  531.3 58.1 %collective-permute-start.15 = (f32[10,1,512]{2,1,0:T(1,128)S(1)}, f32[10,1,512]{2,1,0:T(1,128)S(1)}, u32[]{:S(2)}, u32[]{:S(2)}) collective-permute-start(f32[10,1,512]{2,1,0:T(1,128)S(1)} %get-tuple-element.188), channel_id=1, source_target_pairs={{0,1},{1,2},{2,3},{4,5},{5,6},{6,7},{8,9},{9,10},{10,11},{12,13},{... | collective-permute-start | bytes 61448 | tf_op jit(solution)/shard_map/ppermute | solution.py:22
  668.8 5.4 collective-permute-start.16
  670.1 5.3 collective-permute-start.17
  675.4 7.1 collective-permute-start.18
  678.6 4.7 collective-permute-start.19
  684.3 51.8 %copy-start.2 = (f32[8,32,512]{2,1,0:T(8,128)}, f32[8,32,512]{2,1,0:T(8,128)S(1)}, u32[]{:S(2)}) copy-start(f32[8,32,512]{2,1,0:T(8,128)S(1)} %fusion.26) | copy-start | bytes 1572868
  704.4 4.7 collective-permute-start.20
  806.4 8.1 collective-permute-start.21
  816.7 390.8 %reduce-scatter.19.cloned.1.call-start = ((), (), s32[]{:S(2)}) async-start(), calls=%async_computation.7 | async-start | bytes 7864320
  1030.4 4.3 collective-permute-start.22
  1132.1 6.4 collective-permute-start.23
  (6 other events, 96.1 us)
Sparse Core Ops, SparseCore 0:
  189.0 77.7 reduce-scatter.12
  520.2 66.5 reduce-scatter.14
  816.9 71.0 reduce-scatter.16
  1140.9 66.5 reduce-scatter.18
where the time goes:
time: 1290 us; the launch traced here: 1280 us
  blocking collectives  447 us (35%)
  waiting for transfers between devices  287 us (22%)
  other arithmetic  266 us (21%)
  local copies, waits for them, and re-layouts  191 us (15%)
  starting transfers between devices  68 us (5%)
  between operations  23.2 us (2%)
    psum x6, blocking collectives, global_sums(): totals = lax.psum((values[0],), ('gx', 'gy'))  388 us
    unnamed x8, waiting for transfers between devices  268 us
    scatter-add x4, other arithmetic, one_turn(): return summed.at[:, connect].add(product.reshape(3, node_order, turn_width))  245 us
    gather x8, local copies, waits for them, and re-layouts, one_turn(): gathered = extended[:, connect].reshape(3 * node_order, turn_width)  108 us
    ppermute x8, starting transfers between devices, padded_2(): lax.ppermute(lax.slice_in_dim(block, block.shape[dim] - width, None, axis...  35.2 us
    all_gather x4, blocking collectives, apply_fn(): segment_vec = lax.all_gather(vector_in, 'gy', axis=1, tiled=True)  30.8 us
  transfers between devices with their start and end apart: 28, of which 14 were waited for; matrix products, arithmetic and copies ran while one was open for 2% of the time, Pallas kernels for 0%

commit v1 on v0

--- a/solution.py
+++ b/solution.py
@@ -45,7 +45,7 @@
 
 
 def global_sums(values):
-    totals = lax.psum((values[0],), ("gx", "gy"))
+    totals = lax.psum(lax.psum((values[0],), "gx"), "gy")
     return totals
 
 

time: 1290 us -> 1410 us (1.093)
  blocking collectives: 447 us -> 590 us
  waiting for transfers between devices: 287 us -> 268 us
    psum x6 -> x12, blocking collectives: 388 us -> 532 us  [global_sums(): totals = lax.psum(lax.psum((values[0],), 'gx'), 'gy')]
    unnamed x8, waiting for transfers between devices: 268 us -> 249 us
where the time goes in v1:
time: 1410 us
  blocking collectives  590 us (42%)
  waiting for transfers between devices  268 us (19%)
  other arithmetic  266 us (19%)
  local copies, waits for them, and re-layouts  191 us (14%)
  starting transfers between devices  72.2 us (5%)
  between operations  23 us (2%)
    psum x12, blocking collectives, global_sums(): totals = lax.psum(lax.psum((values[0],), 'gx'), 'gy')  532 us
    unnamed x8, waiting for transfers between devices  249 us
    scatter-add x4, other arithmetic, one_turn(): return summed.at[:, connect].add(product.reshape(3, node_order, turn_width))  245 us
    gather x8, local copies, waits for them, and re-layouts, one_turn(): gathered = extended[:, connect].reshape(3 * node_order, turn_width)  108 us
    ppermute x8, starting transfers between devices, padded_2(): lax.ppermute(lax.slice_in_dim(block, block.shape[dim] - width, None, axis...  35.7 us
    all_gather x4, blocking collectives, apply_fn(): segment_vec = lax.all_gather(vector_in, 'gy', axis=1, tiled=True)  30.1 us
  transfers between devices with their start and end apart: 28, of which 14 were waited for; matrix products, arithmetic and copies ran while one was open for 2% of the time, Pallas kernels for 0%

profile of v1, /device:TPU:1, one launch (start us, length us, event | category | flops | bytes accessed | tf_op | source)
XLA Modules:
  0.0 1412.1 jit_solution(16626982001988713694)
XLA Ops:
  16.6 7.8 all-gather
  46.7 6.8 collective-permute-start.7
  67.9 7.5 all_gather.26
  84.6 22.8 %gather_fusion.2 = f32[10368,3]{1,0:T(8,128)} fusion(f32[3,12544]{0,1:T(8,128)} %copy.164, s32[11264]{0:T(1024)S(1)} %pad_clamp_fusion), kind=kCustom, calls=%fused_computation.2 | custom fusion | bytes 290304 | tf_op jit(solution)/shard_map/while/body/eval_jaxpr/gather | solution.py:99
  115.6 61.1 %scatter_custom_fusion = f32[3,12544]{0,1:T(8,128)} fusion(s32[10368]{0:T(1024)S(1)} %reshape.330, f32[10368,3]{1,0:T(8,128)} %bitcast.64, f32[]{:T(128)} %constant.216.clone.1), kind=kCustom, calls=%fused_computation.18 | custom fusion | flops 31104 | bytes 151040 | tf_op jit(solution)/shard_map/while/body/eval_jaxpr/scatter-add | solution.py:107
  188.9 77.8 %reduce-scatter.13.cloned.1.call-done = f32[3072,3]{1,0:T(8,128)} async-done(((f32[12288,3]{1,0:T(8,128)}), f32[3072,3]{1,0:T(8,128)}) %reduce-scatter.13.cloned.1.call-update) | async-done | bytes 36880
  269.3 68.4 %all-reduce.7 = (f32[]{:T(128)}, f32[]{:T(128)}) all-reduce(f32[]{:T(128)} %get-tuple-element.181, f32[]{:T(128)} %get-tuple-element.180), channel_id=1, replica_groups=mesh['gx'=32,'gy'=4] {'gx'}, use_global_device_ids=true, to_apply=%region_5.6 | all-reduce | flops 2 | bytes 16 | tf_op jit(solution)/shard_map/psum | solution.py:48
  337.7 22.0 %all-reduce.9 = (f32[]{:T(128)}, f32[]{:T(128)}) all-reduce(f32[]{:T(128)} %get-tuple-element.184, f32[]{:T(128)} %get-tuple-element.185), channel_id=1, replica_groups=mesh['gx'=32,'gy'=4] {'gy'}, use_global_device_ids=true, to_apply=%region_6.7 | all-reduce | flops 2 | bytes 16 | tf_op jit(solution)/shard_map/psum | solution.py:48
  361.6 63.5 %psum.116 = f32[]{:T(128)} all-reduce(f32[]{:T(128)} %multiply_reduce_fusion.5), channel_id=1, replica_groups=mesh['gx'=32,'gy'=4] {'gx'}, use_global_device_ids=true, to_apply=%region_14.15 | all-reduce | flops 1 | bytes 8 | tf_op jit(solution)/shard_map/psum | solution.py:48
  425.1 21.7 %psum.117 = f32[]{:T(128)} all-reduce(f32[]{:T(128)} %psum.116), channel_id=1, replica_groups=mesh['gx'=32,'gy'=4] {'gy'}, use_global_device_ids=true, to_apply=%region_15.16 | all-reduce | flops 1 | bytes 8 | tf_op jit(solution)/shard_map/psum | solution.py:48
  448.1 7.6 all_gather.27
  464.6 22.8 %gather_fusion.3 = f32[10368,3]{1,0:T(8,128)} fusion(f32[3,12544]{0,1:T(8,128)} %copy.168, s32[11264]{0:T(1024)S(1)} %pad_clamp_fusion), kind=kCustom, calls=%fused_computation.3 | custom fusion | bytes 290304 | tf_op jit(solution)/shard_map/while/body/eval_jaxpr/gather | solution.py:99
  495.6 61.1 %scatter_custom_fusion.1 = f32[3,12544]{0,1:T(8,128)} fusion(s32[10368]{0:T(1024)S(1)} %reshape.330, f32[10368,3]{1,0:T(8,128)} %bitcast.65, f32[]{:T(128)} %constant.216.clone.1), kind=kCustom, calls=%fused_computation.16 | custom fusion | flops 31104 | bytes 151040 | tf_op jit(solution)/shard_map/while/body/eval_jaxpr/scatter-add | solution.py:107
  582.9 46.7 %reduce-scatter.15.cloned.1.call-done = f32[3072,3]{1,0:T(8,128)} async-done(((f32[12288,3]{1,0:T(8,128)}), f32[3072,3]{1,0:T(8,128)}) %reduce-scatter.15.cloned.1.call-update) | async-done | bytes 36880
  632.2 68.3 %psum.118 = f32[]{:T(128)} all-reduce(f32[]{:T(128)} %multiply_reduce_fusion.4), channel_id=1, replica_groups=mesh['gx'=32,'gy'=4] {'gx'}, use_global_device_ids=true, to_apply=%region_19.20 | all-reduce | flops 1 | bytes 8 | tf_op jit(solution)/shard_map/psum | solution.py:48
  700.9 22.0 %psum.119 = f32[]{:T(128)} all-reduce(f32[]{:T(128)} %psum.118), channel_id=1, replica_groups=mesh['gx'=32,'gy'=4] {'gy'}, use_global_device_ids=true, to_apply=%region_20.0 | all-reduce | flops 1 | bytes 8 | tf_op jit(solution)/shard_map/psum | solution.py:48
  724.4 7.0 all-gather.2
  752.5 7.0 all-gather.3
  764.8 7.5 all_gather.30
  781.2 22.8 %gather_fusion.6 = f32[10368,3]{1,0:T(8,128)} fusion(f32[3,12544]{0,1:T(8,128)} %copy.173, s32[11264]{0:T(1024)S(1)} %pad_clamp_fusion), kind=kCustom, calls=%fused_computation.6 | custom fusion | bytes 290304 | tf_op jit(solution)/shard_map/while/body/eval_jaxpr/gather | solution.py:99
  812.2 61.1 %scatter_custom_fusion.2 = f32[3,12544]{0,1:T(8,128)} fusion(s32[10368]{0:T(1024)S(1)} %reshape.330, f32[10368,3]{1,0:T(8,128)} %bitcast.66, f32[]{:T(128)} %constant.216.clone.1), kind=kCustom, calls=%fused_computation.14 | custom fusion | flops 31104 | bytes 151040 | tf_op jit(solution)/shard_map/while/body/eval_jaxpr/scatter-add | solution.py:107
  884.6 63.1 %reduce-scatter.17.cloned.1.call-done = f32[3072,3]{1,0:T(8,128)} async-done(((f32[12288,3]{1,0:T(8,128)}), f32[3072,3]{1,0:T(8,128)}) %reduce-scatter.17.cloned.1.call-update) | async-done | bytes 36880
  950.3 68.4 %all-reduce.6 = (f32[]{:T(128)}, f32[]{:T(128)}) all-reduce(f32[]{:T(128)} %get-tuple-element.179, f32[]{:T(128)} %get-tuple-element.178), channel_id=1, replica_groups=mesh['gx'=32,'gy'=4] {'gx'}, use_global_device_ids=true, to_apply=%region_25.26 | all-reduce | flops 2 | bytes 16 | tf_op jit(solution)/shard_map/psum | solution.py:48
  1018.7 22.0 %all-reduce.8 = (f32[]{:T(128)}, f32[]{:T(128)}) all-reduce(f32[]{:T(128)} %get-tuple-element.182, f32[]{:T(128)} %get-tuple-element.183), channel_id=1, replica_groups=mesh['gx'=32,'gy'=4] {'gy'}, use_global_device_ids=true, to_apply=%region_26.27 | all-reduce | flops 2 | bytes 16 | tf_op jit(solution)/shard_map/psum | solution.py:48
  1042.6 63.5 %psum.124 = f32[]{:T(128)} all-reduce(f32[]{:T(128)} %multiply_reduce_fusion.1), channel_id=1, replica_groups=mesh['gx'=32,'gy'=4] {'gx'}, use_global_device_ids=true, to_apply=%region_33.34 | all-reduce | flops 1 | bytes 8 | tf_op jit(solution)/shard_map/psum | solution.py:48
  1106.1 21.7 %psum.125 = f32[]{:T(128)} all-reduce(f32[]{:T(128)} %psum.124), channel_id=1, replica_groups=mesh['gx'=32,'gy'=4] {'gy'}, use_global_device_ids=true, to_apply=%region_34.35 | all-reduce | flops 1 | bytes 8 | tf_op jit(solution)/shard_map/psum | solution.py:48
  1129.1 7.6 all_gather.31
  1145.6 22.8 %gather_fusion.7 = f32[10368,3]{1,0:T(8,128)} fusion(f32[3,12544]{0,1:T(8,128)} %copy.177, s32[11264]{0:T(1024)S(1)} %pad_clamp_fusion), kind=kCustom, calls=%fused_computation.7 | custom fusion | bytes 290304 | tf_op jit(solution)/shard_map/while/body/eval_jaxpr/gather | solution.py:99
  1176.6 61.1 %scatter_custom_fusion.3 = f32[3,12544]{0,1:T(8,128)} fusion(s32[10368]{0:T(1024)S(1)} %reshape.330, f32[10368,3]{1,0:T(8,128)} %bitcast.63, f32[]{:T(128)} %constant.216.clone.1), kind=kCustom, calls=%fused_computation.12 | custom fusion | flops 31104 | bytes 151040 | tf_op jit(solution)/shard_map/while/body/eval_jaxpr/scatter-add | solution.py:107
  1248.9 61.7 %reduce-scatter.19.cloned.1.call-done = f32[3072,3]{1,0:T(8,128)} async-done(((f32[12288,3]{1,0:T(8,128)}), f32[3072,3]{1,0:T(8,128)}) %reduce-scatter.19.cloned.1.call-update) | async-done | bytes 36880
  1313.2 68.3 %psum.126 = f32[]{:T(128)} all-reduce(f32[]{:T(128)} %multiply_reduce_fusion), channel_id=1, replica_groups=mesh['gx'=32,'gy'=4] {'gx'}, use_global_device_ids=true, to_apply=%region_38.39 | all-reduce | flops 1 | bytes 8 | tf_op jit(solution)/shard_map/psum | solution.py:48
  1381.5 22.1 %psum.127 = f32[]{:T(128)} all-reduce(f32[]{:T(128)} %psum.126), channel_id=1, replica_groups=mesh['gx'=32,'gy'=4] {'gy'}, use_global_device_ids=true, to_apply=%region_39.40 | all-reduce | flops 1 | bytes 8 | tf_op jit(solution)/shard_map/psum | solution.py:48
  (197 shorter events, 213.6 us)
Async XLA Ops:
  7.2 104.4 %copy-start = (f32[81,81]{1,0:T(8,128)S(1)}, f32[81,81]{1,0:T(8,128)}, u32[]{:S(2)}) copy-start(f32[81,81]{1,0:T(8,128)} %param.31) | copy-start | bytes 78736
  7.2 259.6 %reduce-scatter.13.cloned.1.call-start = ((), (), s32[]{:S(2)}) async-start(), calls=%async_computation.4 | async-start | bytes 7864320
  9.1 20.0 %collective-permute-start = (f32[1,32,512]{2,1,0:T(8,128)S(1)}, f32[1,32,512]{2,1,0:T(8,128)S(1)}, u32[]{:S(2)}, u32[]{:S(2)}) collective-permute-start(f32[1,32,512]{2,1,0:T(8,128)S(1)} %broadcast.217), channel_id=1, source_target_pairs={{4,0},{8,4},{12,8},{16,12},{20,16},{24,20},{28,24},{32,28},{36,32}... | collective-permute-start | bytes 196616 | tf_op jit(solution)/shard_map/ppermute | solution.py:25
  10.4 18.7 %collective-permute-start.1 = (f32[1,32,512]{2,1,0:T(8,128)S(1)}, f32[1,32,512]{2,1,0:T(8,128)S(1)}, u32[]{:S(2)}, u32[]{:S(2)}) collective-permute-start(f32[1,32,512]{2,1,0:T(8,128)S(1)} %broadcast.217), channel_id=1, source_target_pairs={{0,4},{4,8},{8,12},{12,16},{16,20},{20,24},{24,28},{28,32},{32,36}... | collective-permute-start | bytes 196616 | tf_op jit(solution)/shard_map/ppermute | solution.py:22
  29.2 7.4 collective-permute-start.2
  31.3 5.9 collective-permute-start.3
  37.6 39.0 %copy-start.9 = (f32[384]{0:T(512)S(1)}, f32[384]{0:T(512)}, u32[]{:S(2)}) copy-start(f32[384]{0:T(512)} %param.32) | copy-start | bytes 4612
  38.1 5.3 collective-permute-start.4
  39.4 5.3 collective-permute-start.5
  44.8 10.1 collective-permute-start.6
  46.7 8.2 collective-permute-start.7
  75.3 5.0 collective-permute-start.8
  177.6 9.0 collective-permute-start.9
  186.7 82.0 %copy-start.3 = (f32[3072]{0:T(1024)S(1)}, f32[3072]{0:T(1024)}, u32[]{:S(2)}) copy-start(f32[3072]{0:T(1024)} %param.35) | copy-start | bytes 36868
  188.9 440.7 %reduce-scatter.15.cloned.1.call-start = ((), (), s32[]{:S(2)}) async-start(), calls=%async_computation.5 | async-start | bytes 7864320
  455.7 4.6 collective-permute-start.10
  557.6 8.1 collective-permute-start.11
  568.0 379.8 %reduce-scatter.17.cloned.1.call-start = ((), (), s32[]{:S(2)}) async-start(), calls=%async_computation.6 | async-start | bytes 7864320
  568.0 5.3 collective-permute-start.12
  569.3 5.3 collective-permute-start.13
  574.7 125.8 %collective-permute-start.14 = (f32[10,1,512]{2,1,0:T(1,128)S(1)}, f32[10,1,512]{2,1,0:T(1,128)S(1)}, u32[]{:S(2)}, u32[]{:S(2)}) collective-permute-start(f32[10,1,512]{2,1,0:T(1,128)S(1)} %get-tuple-element.193), channel_id=1, source_target_pairs={{1,0},{2,1},{3,2},{5,4},{6,5},{7,6},{9,8},{10,9},{11,10},{13,12},{... | collective-permute-start | bytes 61448 | tf_op jit(solution)/shard_map/ppermute | solution.py:25
  579.3 121.2 %collective-permute-start.15 = (f32[10,1,512]{2,1,0:T(1,128)S(1)}, f32[10,1,512]{2,1,0:T(1,128)S(1)}, u32[]{:S(2)}, u32[]{:S(2)}) collective-permute-start(f32[10,1,512]{2,1,0:T(1,128)S(1)} %get-tuple-element.192), channel_id=1, source_target_pairs={{0,1},{1,2},{2,3},{4,5},{5,6},{6,7},{8,9},{9,10},{10,11},{12,13},{... | collective-permute-start | bytes 61448 | tf_op jit(solution)/shard_map/ppermute | solution.py:22
  736.8 5.4 collective-permute-start.16
  738.1 5.3 collective-permute-start.17
  743.4 7.1 collective-permute-start.18
  746.6 4.7 collective-permute-start.19
  752.3 51.7 %copy-start.2 = (f32[8,32,512]{2,1,0:T(8,128)}, f32[8,32,512]{2,1,0:T(8,128)S(1)}, u32[]{:S(2)}) copy-start(f32[8,32,512]{2,1,0:T(8,128)S(1)} %fusion.26) | copy-start | bytes 1572868
  772.2 4.7 collective-permute-start.20
  874.2 8.1 collective-permute-start.21
  884.6 426.0 %reduce-scatter.19.cloned.1.call-start = ((), (), s32[]{:S(2)}) async-start(), calls=%async_computation.7 | async-start | bytes 7864320
  1136.7 4.6 collective-permute-start.22
  1238.6 8.1 collective-permute-start.23
  (6 other events, 96.1 us)
Sparse Core Ops, SparseCore 0:
  189.0 77.7 reduce-scatter.12
  568.1 61.4 reduce-scatter.14
  884.7 63.0 reduce-scatter.16
  1249.1 61.4 reduce-scatter.18
